TPU v7x, 512 devices: a whole 4x4x16 slice. The times are simulated.
512 devices in a mesh: row: 8 (over y, z_hi), col: 64 (over z_lo, x, core).
Axes of the slice: x: 4, y: 4, z: 16 (z_hi: 2, z_lo: 8; z = z_hi * 8 + z_lo), core: 2. Of those that a mesh axis runs over, the one named last changes fastest.
Arguments:
- side_a: float32 [64, 8192], P('row', 'col'), may hold values from -6 to 6
- side_b: float32 [2048, 8192], P('col', 'row'), may hold values from -6 to 6
- pair_grad: float32 [64, 2048, 128], P('row', 'col'), may hold values from -6 to 6
- out_weight: float32 [1024, 128], replicated, may hold values from -0.1875 to 0.1875
Outputs:
- grad_a: float32 [64, 8192], P('row', 'col')
- grad_b: float32 [2048, 8192], P('col', 'row')
- grad_weight: float32 [1024, 128], replicated
- grad_bias: float32 [128], replicated
All inputs are finite; a program needn't handle non-finite values.
Results may differ from a plain program's by a relative error of at most 0.00013.
Values sent between devices are 32-bit elements; how exact they have to be, the bound alone decides.
A program may use at most 64 MiB of HBM per device.

v0:
```python
import jax
import jax.numpy as jnp
from jax import lax
from jax.sharding import PartitionSpec as P

S = 256
C = 32
P_SIZE = 128


def local(side_a, side_b, pair_grad, out_weight):
    high = lax.Precision.HIGHEST
    rows = pair_grad.shape[0]
    cols = pair_grad.shape[1]
    left = lax.all_gather(side_a, "col", axis=1, tiled=True).reshape(rows, S, C)
    right = lax.all_gather(side_b, "row", axis=1, tiled=True).reshape(cols, S, C)
    left_flat = jnp.transpose(left, (0, 2, 1)).reshape(rows * C, S)
    right_flat = jnp.transpose(right, (1, 0, 2)).reshape(S, cols * C)
    flat_pair = pair_grad.reshape(rows * cols, P_SIZE)
    grad_outer = jnp.dot(flat_pair, out_weight.T, precision=high)
    grad_tile = jnp.transpose(grad_outer.reshape(rows, cols, C, C), (0, 2, 1, 3)).reshape(
        rows * C, cols * C
    )
    left_grad = jnp.dot(grad_tile, right_flat.T, precision=high) / S
    left_part = jnp.transpose(left_grad.reshape(rows, C, S), (0, 2, 1)).reshape(rows, S * C)
    right_grad = jnp.dot(left_flat.T, grad_tile, precision=high) / S
    right_part = jnp.transpose(right_grad.reshape(S, cols, C), (1, 0, 2)).reshape(cols, S * C)
    left_total = lax.psum(left_part, "col")
    right_total = lax.psum(right_part, "row")
    left_width = side_a.shape[1]
    right_width = side_b.shape[1]
    grad_a = lax.dynamic_slice_in_dim(left_total, lax.axis_index("col") * left_width, left_width, 1)
    grad_b = lax.dynamic_slice_in_dim(
        right_total, lax.axis_index("row") * right_width, right_width, 1
    )
    outer = jnp.dot(left_flat, right_flat, precision=high) / S
    outer = jnp.transpose(outer.reshape(rows, C, cols, C), (0, 2, 1, 3)).reshape(rows * cols, C * C)
    weight_part = jnp.dot(outer.T, flat_pair, precision=high)
    bias_part = jnp.sum(flat_pair, axis=0)
    weight_sums = lax.psum((weight_part, bias_part), ("row", "col"))
    return (grad_a, grad_b, weight_sums[0], weight_sums[1])


def solution(mesh):
    in_specs = (P("row", "col"), P("col", "row"), P("row", "col", None), P())
    out_specs = (P("row", "col"), P("col", "row"), P(), P())
    return jax.shard_map(local, mesh=mesh, in_specs=in_specs, out_specs=out_specs, check_vma=False)
```

profile of v0, /device:TPU:4, one launch (start us, length us, event | category | flops | bytes accessed | tf_op | source)
XLA Modules:
  0.0 1648.9 jit_solution(14450162567662222692)
XLA Ops:
  7.2 0.0 copy-start
  7.2 0.0 all-gather.2.cloned.1.call-start
  7.2 0.7 all-gather.2.cloned.1.call-update
  7.9 0.0 all-reduce.6.cloned.1.call-start
  8.0 0.3 copy-done
  8.2 0.0 copy-start.2
  8.2 5.9 convolution_bitcast_fusion
  14.1 3.7 reshape.48
  17.9 0.0 copy-done.2
  17.9 119.1 %all_gather.7 = f32[8,8192]{1,0:T(8,128)S(1)} all-gather(f32[8,128]{1,0:T(8,128)S(1)} %copy-done.2), channel_id=1, replica_groups=mesh['row'=8,'col'=64] {'col'}, dimensions={1}, use_global_device_ids=true | all-gather | bytes 266240 | tf_op jit(solution)/shard_map/all_gather | solution.py:15
  137.0 0.3 reshape.53
  137.3 0.3 copy.12
  137.6 1.8 convolution_multiply_fusion.1
  139.5 2.6 copy.13
  142.1 4.4 reshape.56
  146.5 0.0 all-reduce.6.cloned.1.call-update
  146.5 0.2 all-reduce.4.cloned.1.call-start
  146.8 0.0 all-gather.2.cloned.1.call-done
  146.8 3.7 reshape.49
  150.5 2.8 copy.10
  153.3 1.0 convolution_multiply_fusion.2
  154.4 0.3 copy.11
  154.7 1.2 reshape.52
  155.9 1.0 convolution_multiply_fusion
  157.0 2.7 reshape.57
  159.7 6.5 copy.17
  166.2 0.0 copy-start.1
  166.2 3.8 reshape.58
  170.0 0.0 all-reduce.4.cloned.1.call-update
  170.0 0.0 all-reduce.8.cloned.1.call-start
  170.1 0.0 copy-done.1
  170.1 2.6 fusion.1
  172.7 0.0 all-reduce.8.cloned.1.call-update
  172.7 0.1 reduce_sum.9
  172.8 158.6 %psum.31 = f32[128]{0:T(128)} all-reduce(f32[128]{0:T(128)S(1)} %reduce_sum.9), channel_id=1, replica_groups=mesh['row'=8,'col'=64] {'row','col'}, use_global_device_ids=true, to_apply=%region_4.0 | all-reduce | flops 128 | bytes 1024 | tf_op jit(solution)/shard_map/psum | solution.py:40
  331.4 64.2 %all-reduce.6.cloned.1.call-done = f32[32,8192]{1,0:T(8,128)} async-done(((f32[32,8192]{1,0:T(8,128)}), f32[32,8192]{1,0:T(8,128)}) %all-reduce.6.cloned.1.call-update) | async-done | bytes 1048592 | tf_op jit(solution)/shard_map/psum | solution.py:29
  395.6 1.6 constant_dynamic-slice_fusion
  397.2 767.8 %all-reduce.4.cloned.1.call-done = f32[8,8192]{1,0:T(8,128)} async-done(((f32[8,8192]{1,0:T(8,128)}), f32[8,8192]{1,0:T(8,128)}) %all-reduce.4.cloned.1.call-update) | async-done | bytes 262160 | tf_op jit(solution)/shard_map/psum | solution.py:28
  1165.0 1.3 constant_dynamic-slice_fusion.1
  1166.3 474.2 %all-reduce.8.cloned.1.call-done = f32[1024,128]{1,0:T(8,128)} async-done(((f32[1024,128]{1,0:T(8,128)}), f32[1024,128]{1,0:T(8,128)}) %all-reduce.8.cloned.1.call-update) | async-done | bytes 524304 | tf_op jit(solution)/shard_map/psum | solution.py:40
  1640.5 1.9 copy.21
Async XLA Ops:
  7.2 1.0 copy-start
  7.2 139.6 %all-gather.2.cloned.1.call-start = ((), (), s32[]{:S(2)}) async-start(), calls=%async_computation | async-start | bytes 1179648 | tf_op jit(solution)/shard_map/all_gather | solution.py:16
  7.9 387.7 %all-reduce.6.cloned.1.call-start = ((), (), s32[]{:S(2)}) async-start(), calls=%async_computation.2 | async-start | bytes 2097152 | tf_op jit(solution)/shard_map/psum | solution.py:29
  8.2 9.7 copy-start.2
  146.5 1018.5 %all-reduce.4.cloned.1.call-start = ((), (), s32[]{:S(2)}) async-start(), calls=%async_computation.1 | async-start | bytes 524288 | tf_op jit(solution)/shard_map/psum | solution.py:28
  166.2 3.9 copy-start.1
  170.0 1470.4 %all-reduce.8.cloned.1.call-start = ((), (), s32[]{:S(2)}) async-start(), calls=%async_computation.3 | async-start | bytes 1048576 | tf_op jit(solution)/shard_map/psum | solution.py:40
Sparse Core Ops, SparseCore 0:
  11.2 95.5 all-gather.1
  146.6 248.9 all-reduce.5
  398.5 766.4 all-reduce.3
  1171.8 468.6 all-reduce.7
where the time goes:
time: 1650 us
  waiting for transfers between devices  1310 us (79%)
  blocking collectives  278 us (17%)
  local copies, waits for them, and re-layouts  37.5 us (2%)
    psum x1, waiting for transfers between devices, local(): left_total = lax.psum(left_part, 'col')  768 us
    psum x1, waiting for transfers between devices, local(): weight_sums = lax.psum((weight_part, bias_part), ('row', 'col'))  474 us
    psum x1, blocking collectives, local(): weight_sums = lax.psum((weight_part, bias_part), ('row', 'col'))  159 us
    all_gather x1, blocking collectives, local(): left = lax.all_gather(side_a, 'col', axis=1, tiled=True).reshape(rows, S, C)  119 us
    psum x1, waiting for transfers between devices, local(): right_total = lax.psum(right_part, 'row')  64.2 us
  transfers between devices with their start and end apart: 4, of which 3 were waited for; matrix products, arithmetic and copies ran while one was open for 3% of the time, Pallas kernels for 0%

commit v1 on v0

--- a/solution.py
+++ b/solution.py
@@ -37,7 +37,9 @@
     outer = jnp.transpose(outer.reshape(rows, C, cols, C), (0, 2, 1, 3)).reshape(rows * cols, C * C)
     weight_part = jnp.dot(outer.T, flat_pair, precision=high)
     bias_part = jnp.sum(flat_pair, axis=0)
-    weight_sums = lax.psum((weight_part, bias_part), ("row", "col"))
+    weight_sums = (weight_part, bias_part)
+    for mesh_axis in ("row", "col"):
+        weight_sums = lax.psum(weight_sums, mesh_axis)
     return (grad_a, grad_b, weight_sums[0], weight_sums[1])
 
 

time: 1650 us -> 1310 us (0.79)
  the two profiles are of different devices: /device:TPU:4 before, /device:TPU:8 now
where the time goes in v1:
time: 1310 us
  waiting for transfers between devices  853 us (65%)
  blocking collectives  389 us (30%)
  local copies, waits for them, and re-layouts  39.3 us (3%)
  matrix products  14.6 us (1%)
  between operations  13.8 us (1%)
    psum x1, waiting for transfers between devices, local(): left_total = lax.psum(left_part, 'col')  561 us
    psum x1, waiting for transfers between devices, local(): weight_sums = lax.psum(weight_sums, mesh_axis)  292 us
    psum x2, blocking collectives, local(): weight_sums = lax.psum(weight_sums, mesh_axis)  253 us
    all_gather x1, blocking collectives, local(): left = lax.all_gather(side_a, 'col', axis=1, tiled=True).reshape(rows, S, C)  136 us
  transfers between devices with their start and end apart: 3, of which 2 were waited for; matrix products, arithmetic and copies ran while one was open for 2% of the time, Pallas kernels for 0%

profile of v1, /device:TPU:8, one launch (start us, length us, event | category | flops | bytes accessed | tf_op | source)
XLA Modules:
  0.0 1309.9 jit_solution(11231832324733738134)
XLA Ops:
  7.2 0.0 copy-start
  7.2 0.0 all-gather.2.cloned.1.call-start
  7.2 0.7 all-gather.2.cloned.1.call-update
  7.9 0.0 all-reduce.7.cloned.1.call-start
  8.0 135.9 %all_gather.7 = f32[8,8192]{1,0:T(8,128)S(1)} all-gather(f32[8,128]{1,0:T(8,128)} %param.4), channel_id=1, replica_groups=mesh['row'=8,'col'=64] {'col'}, dimensions={1}, use_global_device_ids=true | all-gather | bytes 266240 | tf_op jit(solution)/shard_map/all_gather | solution.py:15
  143.9 0.3 reshape.53
  144.2 0.3 copy.12
  144.6 0.0 copy-done
  144.6 5.9 convolution_bitcast_fusion
  150.5 3.7 reshape.48
  154.2 1.8 convolution_multiply_fusion.1
  156.1 2.6 copy.13
  158.7 4.4 reshape.56
  163.1 0.0 all-gather.2.cloned.1.call-done
  163.1 3.7 reshape.49
  166.8 2.8 copy.10
  169.6 2.0 convolution_multiply_fusion
  171.6 3.9 reshape.57
  175.6 6.5 copy.17
  182.1 0.0 copy-start.1
  182.1 4.6 reshape.58
  186.7 0.0 copy-done.1
  186.7 3.8 fusion.1
  190.5 0.0 all-reduce.7.cloned.1.call-update
  190.6 0.0 all-reduce.5.cloned.1.call-start
  190.6 1.0 convolution_multiply_fusion.2
  191.6 0.3 copy.11
  192.0 1.2 reshape.52
  193.2 291.8 %all-reduce.7.cloned.1.call-done = (f32[1024,128]{1,0:T(8,128)}, f32[32,8192]{1,0:T(8,128)}) async-done(((f32[1024,128]{1,0:T(8,128)}, f32[32,8192]{1,0:T(8,128)}), (f32[1024,128]{1,0:T(8,128)}, f32[32,8192]{1,0:T(8,128)})) %all-reduce.7.cloned.1.call-update) | async-done | bytes 1572880 | tf_op jit(solution)/shard_map/psum | solution.py:42
  485.0 0.0 all-reduce.5.cloned.1.call-update
  485.0 0.1 reduce_sum.9
  485.1 41.9 %psum.46 = f32[128]{0:T(128)S(1)} all-reduce(f32[128]{0:T(128)S(1)} %reduce_sum.9), channel_id=1, replica_groups=mesh['row'=8,'col'=64] {'row'}, use_global_device_ids=true, to_apply=%region_5.0 | all-reduce | flops 128 | bytes 1024 | tf_op jit(solution)/shard_map/psum | solution.py:42
  527.0 210.8 %psum.47 = f32[128]{0:T(128)} all-reduce(f32[128]{0:T(128)S(1)} %psum.46), channel_id=1, replica_groups=mesh['row'=8,'col'=64] {'col'}, use_global_device_ids=true, to_apply=%region_6.0 | all-reduce | flops 128 | bytes 1024 | tf_op jit(solution)/shard_map/psum | solution.py:42
  737.8 1.6 constant_dynamic-slice_fusion
  739.4 560.8 %all-reduce.5.cloned.1.call-done = (f32[8,8192]{1,0:T(8,128)}, f32[1024,128]{1,0:T(8,128)}) async-done(((f32[8,8192]{1,0:T(8,128)}, f32[1024,128]{1,0:T(8,128)}), (f32[8,8192]{1,0:T(8,128)}, f32[1024,128]{1,0:T(8,128)})) %all-reduce.5.cloned.1.call-update) | async-done | bytes 786448 | tf_op jit(solution)/shard_map/psum | solution.py:28
  1300.2 1.3 constant_dynamic-slice_fusion.1
  1301.5 1.9 copy.22
Async XLA Ops:
  7.2 137.4 %copy-start = (f32[1024,128]{1,0:T(8,128)S(1)}, f32[1024,128]{1,0:T(8,128)}, u32[]{:S(2)}) copy-start(f32[1024,128]{1,0:T(8,128)} %param.7) | copy-start | bytes 1572868
  7.2 155.9 %all-gather.2.cloned.1.call-start = ((), (), s32[]{:S(2)}) async-start(), calls=%async_computation | async-start | bytes 1179648 | tf_op jit(solution)/shard_map/all_gather | solution.py:16
  7.9 477.1 %all-reduce.7.cloned.1.call-start = ((), (), s32[]{:S(2)}) async-start(), calls=%async_computation.2 | async-start | bytes 3145728 | tf_op jit(solution)/shard_map/psum | solution.py:42
  182.1 4.6 copy-start.1
  190.6 1109.7 %all-reduce.5.cloned.1.call-start = ((), (), s32[]{:S(2)}) async-start(), calls=%async_computation.1 | async-start | bytes 1572864 | tf_op jit(solution)/shard_map/psum | solution.py:28
Sparse Core Ops, SparseCore 0:
  11.2 95.3 all-gather.1
  190.7 294.2 all-reduce.6
  488.0 812.2 all-reduce.4
